TPU v7x, 256 devices: a whole 4x4x8 slice. The times are simulated.
256 devices in a mesh: dp: 128 (over z, x, y_hi, core), mp: 2 (over y_lo).
Axes of the slice: x: 4, y: 4 (y_hi: 2, y_lo: 2; y = y_hi * 2 + y_lo), z: 8, core: 2. Of those that a mesh axis runs over, the one named last changes fastest.
Arguments:
- features: bfloat16 [256, 512, 768], P('dp'), may hold values from -24 to 24
- patch_counts: int32 [256], P('dp'), may hold values from 216 to 512, as said below
- ln1_gain: float32 [768], replicated, may hold values from 0.25 to 1.75
- ln1_bias: float32 [768], replicated, may hold values from -1.5 to 1.5
- query_key_value_weight: bfloat16 [768, 3, 768], P('dp', None, 'mp'), may hold values from -0.21875 to 0.21875
- qv_bias: float32 [2, 768], P(None, 'mp'), may hold values from -1.5 to 1.5
- out_weight: bfloat16 [768, 768], P('mp', 'dp'), may hold values from -3 to 3
- out_bias: float32 [768], replicated, may hold values from -1.5 to 1.5
- ln2_gain: float32 [768], replicated, may hold values from 0.25 to 1.75
- ln2_bias: float32 [768], replicated, may hold values from -1.5 to 1.5
- fc1_weight: bfloat16 [768, 3072], P('dp', 'mp'), may hold values from -0.21875 to 0.21875
- fc1_bias: float32 [3072], P('mp'), may hold values from -1.5 to 1.5
- fc2_weight: bfloat16 [3072, 768], P('mp', 'dp'), may hold values from -0.109375 to 0.109375
- fc2_bias: float32 [768], replicated, may hold values from -1.5 to 1.5
- cotangent: bfloat16 [256, 512, 768], P('dp'), may hold values from -24 to 24
Outputs:
- layer_out: bfloat16 [256, 512, 768], P('dp')
- features_grad: float32 [256, 512, 768], P('dp')
- ln1_gain_grad: float32 [768], replicated
- ln1_bias_grad: float32 [768], replicated
- qkv_weight_grad: float32 [768, 3, 768], P('dp', None, 'mp')
- qv_bias_grad: float32 [2, 768], P(None, 'mp')
- out_weight_grad: float32 [768, 768], P('mp', 'dp')
- out_bias_grad: float32 [768], replicated
- ln2_gain_grad: float32 [768], replicated
- ln2_bias_grad: float32 [768], replicated
- fc1_weight_grad: float32 [768, 3072], P('dp', 'mp')
- fc1_bias_grad: float32 [3072], P('mp')
- fc2_weight_grad: float32 [3072, 768], P('mp', 'dp')
- fc2_bias_grad: float32 [768], replicated
Inputs may be any that keep to these rules, and one draw needn't show every extreme that they name: `patch_counts`: each item has 216, 256 or 512 valid patches, the first ones of its slots; both the smallest and the largest occur in every draw.
All inputs are finite; a program needn't handle non-finite values.
Results may differ from a plain program's by a relative error of at most 0.012.
Values may be sent and summed in bfloat16 or wider, within the bound.
No kernel may reach another device: no remote copies, remote signals or barrier semaphores. Data moves between devices by JAX's collectives and lax.ppermute only.
A program may use at most 128 MiB of HBM per device.

v0:
```python
from functools import partial
import math

import jax
import jax.numpy as jnp
from jax import lax
from jax.sharding import PartitionSpec as P

DH = 64


norm_eps = 1e-06
masked_score = -1e30


def normalize(values):
    row_mean = jnp.mean(values, axis=-1, keepdims=True)
    centred = values - row_mean
    inv_std = lax.rsqrt(jnp.mean(centred * centred, axis=-1, keepdims=True) + norm_eps)
    return (centred * inv_std, inv_std)


def norm_back(grad_normed, gain_row, scaled, inv_std):
    grad_scaled = grad_normed * gain_row
    first_mean = jnp.mean(grad_scaled, axis=-1, keepdims=True)
    second_mean = jnp.mean(grad_scaled * scaled, axis=-1, keepdims=True)
    return inv_std * (grad_scaled - first_mean - scaled * second_mean)


def masked_scores(query_item, key_item, patch_count, score_scale):
    scores = (
        jnp.einsum("qhe,khe->hqk", query_item, key_item, preferred_element_type=jnp.float32)
        * score_scale
    )
    key_valid = jnp.arange(key_item.shape[0]) < patch_count
    return jnp.where(key_valid[None, None, :], scores, masked_score)


def attend_item(pieces, score_scale):
    query_item, key_item, value_item, patch_count = pieces
    scores = masked_scores(query_item, key_item, patch_count, score_scale)
    row_max = jnp.max(scores, axis=-1, keepdims=True)
    shifted = jnp.exp(scores - row_max)
    denom_sum = jnp.sum(shifted, axis=-1, keepdims=True)
    attn_prob = shifted / denom_sum
    context = jnp.einsum(
        "hqk,khe->qhe",
        attn_prob.astype(jnp.bfloat16),
        value_item,
        preferred_element_type=jnp.float32,
    )
    return (context.astype(jnp.bfloat16), row_max + jnp.log(denom_sum))


def attend_back(pieces, score_scale):
    query_item, key_item, value_item, grad_item, log_total, patch_count = pieces
    scores = masked_scores(query_item, key_item, patch_count, score_scale)
    attn_prob = jnp.exp(scores - log_total)
    grad_prob = jnp.einsum(
        "qhe,khe->hqk", grad_item, value_item, preferred_element_type=jnp.float32
    )
    grad_scores = attn_prob * (grad_prob - jnp.sum(attn_prob * grad_prob, axis=-1, keepdims=True))
    grad_low = grad_scores.astype(jnp.bfloat16)
    grad_query = (
        jnp.einsum("hqk,khe->qhe", grad_low, key_item, preferred_element_type=jnp.float32)
        * score_scale
    )
    grad_key = (
        jnp.einsum("hqk,qhe->khe", grad_low, query_item, preferred_element_type=jnp.float32)
        * score_scale
    )
    grad_value = jnp.einsum(
        "hqk,qhe->khe",
        attn_prob.astype(jnp.bfloat16),
        grad_item,
        preferred_element_type=jnp.float32,
    )
    return jnp.stack([grad_query, grad_key, grad_value], axis=1).astype(jnp.bfloat16)


def on_device(
    features,
    patch_counts,
    ln1_gain,
    ln1_bias,
    query_key_value_weight,
    qv_bias,
    out_weight,
    out_bias,
    ln2_gain,
    ln2_bias,
    fc1_weight,
    fc1_bias,
    fc2_weight,
    fc2_bias,
    cotangent,
):
    item_count, token_len, model_width = features.shape
    row_count = item_count * token_len
    inner_width = qv_bias.shape[1]
    head_count = inner_width // DH
    score_scale = 1.0 / math.sqrt(DH)
    feature_rows = features.reshape(row_count, model_width).astype(jnp.float32)
    scaled_one, inv_one = normalize(feature_rows)
    first_normalized = (scaled_one * ln1_gain + ln1_bias).astype(jnp.bfloat16)
    query_key_value_complete, out_full = (
        lax.all_gather(query_key_value_weight, "dp", axis=0, tiled=True),
        lax.all_gather(out_weight, "dp", axis=1, tiled=True),
    )
    projected_rows = jnp.einsum(
        "gq,qzt->gzt",
        first_normalized,
        query_key_value_complete,
        preferred_element_type=jnp.float32,
    )
    bias_row_block = jnp.stack([qv_bias[0], jnp.zeros_like(qv_bias[0]), qv_bias[1]])
    qkv_items = (
        (projected_rows + bias_row_block)
        .astype(jnp.bfloat16)
        .reshape(item_count, token_len, 3, head_count, DH)
    )
    query_all = qkv_items[:, :, 0]
    key_all = qkv_items[:, :, 1]
    value_all = qkv_items[:, :, 2]
    context, log_total = lax.map(
        partial(attend_item, score_scale=score_scale), (query_all, key_all, value_all, patch_counts)
    )
    context_rows = context.reshape(row_count, inner_width)
    branch_part = jnp.dot(context_rows, out_full, preferred_element_type=jnp.float32)
    mid = feature_rows + lax.psum(branch_part, "mp") + out_bias
    scaled_two, inv_two = normalize(mid)
    normed_two = (scaled_two * ln2_gain + ln2_bias).astype(jnp.bfloat16)
    fc1_full, fc2_full = (
        lax.all_gather(fc1_weight, "dp", axis=0, tiled=True),
        lax.all_gather(fc2_weight, "dp", axis=1, tiled=True),
    )
    hidden = jnp.dot(normed_two, fc1_full, preferred_element_type=jnp.float32) + fc1_bias
    active, gelu_pull = jax.vjp(partial(jax.nn.gelu, approximate=False), hidden)
    active_low = active.astype(jnp.bfloat16)
    mlp_part = jnp.dot(active_low, fc2_full, preferred_element_type=jnp.float32)
    result_rows = mid + lax.psum(mlp_part.astype(jnp.bfloat16), "mp").astype(jnp.float32) + fc2_bias
    out_rows = result_rows.astype(jnp.bfloat16)
    layer_out = out_rows.reshape(item_count, token_len, model_width)
    grad_mlp = cotangent.reshape(row_count, model_width)
    fc1_back, fc2_back = (
        lax.all_gather(fc1_weight, "dp", axis=0, tiled=True),
        lax.all_gather(fc2_weight, "dp", axis=1, tiled=True),
    )
    grad_active = jnp.einsum("rd,fd->rf", grad_mlp, fc2_back, preferred_element_type=jnp.float32)
    grad_hidden = gelu_pull(grad_active)[0].astype(jnp.bfloat16)
    fc2_local = jnp.einsum("rf,rd->fd", active_low, grad_mlp, preferred_element_type=jnp.float32)
    fc1_local = jnp.einsum("rd,rf->df", normed_two, grad_hidden, preferred_element_type=jnp.float32)
    normed_two_part = jnp.einsum(
        "rf,df->rd", grad_hidden, fc1_back, preferred_element_type=jnp.float32
    )
    grad_normed_two = lax.psum(normed_two_part, "mp")
    fc1_grad, fc2_grad = (
        lax.psum_scatter(fc1_local, "dp", scatter_dimension=0, tiled=True),
        lax.psum_scatter(fc2_local, "dp", scatter_dimension=1, tiled=True),
    )
    grad_mid = grad_mlp.astype(jnp.float32) + norm_back(
        grad_normed_two, ln2_gain, scaled_two, inv_two
    )
    grad_branch = grad_mid.astype(jnp.bfloat16)
    query_key_value_backward, out_back = (
        lax.all_gather(query_key_value_weight, "dp", axis=0, tiled=True),
        lax.all_gather(out_weight, "dp", axis=1, tiled=True),
    )
    out_local = jnp.einsum(
        "ri,rd->id", context_rows, grad_branch, preferred_element_type=jnp.float32
    )
    grad_context = jnp.einsum(
        "rd,id->ri", grad_branch, out_back, preferred_element_type=jnp.float32
    ).astype(jnp.bfloat16)
    grad_items = grad_context.reshape(item_count, token_len, head_count, DH)
    grad_qkv = lax.map(
        partial(attend_back, score_scale=score_scale),
        (query_all, key_all, value_all, grad_items, log_total, patch_counts),
    )
    projection_gradient = grad_qkv.reshape(row_count, 3, inner_width)
    query_key_value_slice = jnp.einsum(
        "so,sjz->ojz", first_normalized, projection_gradient, preferred_element_type=jnp.float32
    )
    normed_one_part = jnp.einsum(
        "hop,nop->hn",
        projection_gradient,
        query_key_value_backward,
        preferred_element_type=jnp.float32,
    )
    grad_normed_one = lax.psum(normed_one_part.astype(jnp.bfloat16), "mp").astype(jnp.float32)
    qkv_grad, out_grad = (
        lax.psum_scatter(query_key_value_slice, "dp", scatter_dimension=0, tiled=True),
        lax.psum_scatter(out_local, "dp", scatter_dimension=1, tiled=True),
    )
    features_grad = grad_mid + norm_back(grad_normed_one, ln1_gain, scaled_one, inv_one)
    proj_sums = jnp.sum(projection_gradient, axis=0, dtype=jnp.float32)
    small_sums = lax.psum(
        (
            jnp.sum(grad_normed_one * scaled_one, axis=0),
            jnp.sum(grad_normed_one, axis=0),
            jnp.stack([proj_sums[0], proj_sums[2]]),
            jnp.sum(grad_branch, axis=0, dtype=jnp.float32),
            jnp.sum(grad_normed_two * scaled_two, axis=0),
            jnp.sum(grad_normed_two, axis=0),
            jnp.sum(grad_hidden, axis=0, dtype=jnp.float32),
            jnp.sum(grad_mlp, axis=0, dtype=jnp.float32),
        ),
        "dp",
    )
    (
        ln1_gain_grad,
        ln1_bias_grad,
        qv_bias_grad,
        out_bias_grad,
        ln2_gain_grad,
        ln2_bias_grad,
        fc1_bias_grad,
        fc2_bias_grad,
    ) = small_sums
    return (
        layer_out,
        features_grad.reshape(item_count, token_len, model_width),
        ln1_gain_grad,
        ln1_bias_grad,
        qkv_grad,
        qv_bias_grad,
        out_grad,
        out_bias_grad,
        ln2_gain_grad,
        ln2_bias_grad,
        fc1_grad,
        fc1_bias_grad,
        fc2_grad,
        fc2_bias_grad,
    )


def solution(mesh):
    return jax.shard_map(
        on_device,
        mesh=mesh,
        in_specs=(
            P("dp", None, None),
            P("dp"),
            P(),
            P(),
            P("dp", None, "mp"),
            P(None, "mp"),
            P("mp", "dp"),
            P(),
            P(),
            P(),
            P("dp", "mp"),
            P("mp"),
            P("mp", "dp"),
            P(),
            P("dp", None, None),
        ),
        out_specs=(
            P("dp", None, None),
            P("dp", None, None),
            P(),
            P(),
            P("dp", None, "mp"),
            P(None, "mp"),
            P("mp", "dp"),
            P(),
            P(),
            P(),
            P("dp", "mp"),
            P("mp"),
            P("mp", "dp"),
            P(),
        ),
        check_vma=False,
    )
```

profile of v0, /device:TPU:1, one launch (start us, length us, event | category | flops | bytes accessed | tf_op | source)
XLA Modules:
  0.0 2077.2 jit_solution(8521255489611584269)
XLA Ops:
  13.9 189.2 %all-gather = bf16[128,6,384]{2,1,0:T(8,128)(2,1)S(1)} all-gather(bf16[1,6,384]{2,1,0:T(8,128)(2,1)S(1)} %bitcast.208), channel_id=1, replica_groups=mesh['dp'=128,'mp'=2] {'dp'}, dimensions={0}, use_global_device_ids=true | all-gather | bytes 594432 | tf_op jit(solution)/shard_map/all_gather | solution.py:108
  206.1 4.4 add_convert_fusion.1
  213.1 5.6 reshape.222
  221.1 13.5 while.22
  240.1 8.3 all-gather.9.cloned.1.call-done
  248.4 5.3 reshape.233
  253.6 111.9 %all-gather.11.cloned.1.call-done = bf16[128,6,1536]{2,1,0:T(8,128)(2,1)} async-done(((bf16[1,6,1536]{2,1,0:T(8,128)(2,1)}), bf16[128,6,1536]{2,1,0:T(8,128)(2,1)}) %all-gather.11.cloned.1.call-update) | async-done | bytes 2359312 | tf_op jit(solution)/shard_map/all_gather | solution.py:135
  365.6 5.0 reshape.235
  370.6 91.8 %all-reduce.15.cloned.1.call-done = f32[1024,768]{1,0:T(8,128)} async-done(((f32[1024,768]{1,0:T(8,128)}), f32[1024,768]{1,0:T(8,128)}) %all-reduce.15.cloned.1.call-update) | async-done | bytes 3145744 | tf_op jit(solution)/shard_map/psum | solution.py:130
  469.8 19.0 convert_reduce_fusion
  490.4 4.3 fusion.100
  494.7 6.4 multiply_convert_fusion.1
  502.8 4.1 convolution_convert_fusion
  507.0 86.4 %all-reduce.17.cloned.1.call-done = f32[1024,768]{1,0:T(8,128)} async-done(((f32[1024,768]{1,0:T(8,128)}), f32[1024,768]{1,0:T(8,128)}) %all-reduce.17.cloned.1.call-update) | async-done | bytes 3145744 | tf_op jit(solution)/shard_map/psum | solution.py:156
  593.3 3.7 multiply_reduce_fusion.1
  604.5 3.2 reshape.226
  610.0 26.0 %while.23 = (s32[]{:T(128)}, bf16[2,512,3,6,64]{1,4,3,2,0:T(8,128)(2,1)}, bf16[2,512,6,64]{1,3,2,0:T(8,128)(2,1)}, s32[2]{0:T(128)S(1)}, bf16[2,512,6,64]{1,3,2,...) while((s32[]{:T(128)}, ...), condition=%wide.region_15.16_spmd, body=%wide.region_13.15_spmd.sunk | while | flops 1034745344 | bytes 66159340 | solution.py:176
  636.0 5.5 copy.75
  641.5 6.6 reshape.227
  648.0 5.8 bitcast_convert_fusion
  656.7 6.6 fusion.102
  663.3 4.7 fusion.90
  670.0 4.0 fusion.101
  674.1 372.9 %fusion.92 = (f32[8,1536]{1,0:T(8,128)S(1)}, f32[1536,8]{0,1:T(8,128)S(1)}) fusion(f32[768,1536]{1,0:T(8,128)} %fusion.90, f32[1536,768]{0,1:T(8,128)} %fusion.102), kind=kCustom, calls=%all-reduce-scatter.2 | all-reduce-scatter fusion | flops 3145729 | bytes 9536512
  1047.0 5.3 collective-permute-start.32
  1054.9 4.1 collective-permute-start.31
  1064.3 7.0 collective-permute-start.38
  1071.3 16.3 collective-permute-start.39
  1087.7 4.3 collective-permute-start.40
  1093.7 5.5 collective-permute-start.42
  1099.2 5.2 collective-permute-start.43
  1106.0 6.0 collective-permute-start.45
  1114.8 6.2 collective-permute-start.48
  1148.8 4.2 collective-permute-start
  1153.0 5.9 collective-permute-start.1
  1161.6 5.0 collective-permute-start.12
  1166.6 4.3 collective-permute-start.13
  1182.3 4.0 collective-permute-start.2
  1186.3 4.1 collective-permute-start.20
  1196.0 3.7 collective-permute-start.24
  1213.1 4.0 collective-permute-start.4
  1217.2 4.1 collective-permute-start.5
  1224.3 3.3 collective-permute-start.7
  1227.6 8.5 collective-permute-start.8
  1242.7 49.1 %concatenate.9 = f32[1536,262]{0,1:T(8,128)} concatenate(f32[1536,6]{0,1:T(8,128)S(1)} %collective-permute-done.63, f32[1536,8]{0,1:T(8,128)} %copy-done.61, f32[1536,8]{0,1:T(8,128)} %copy-done.59, f32[1536,8]{0,1:T(8,128)} %copy-done.57, f32[1536,8]{0,1:T(8,128)} %copy-done.56, f32[1536,8]{0,1:T(8,128)} %copy-done.55, f32[1536,8]{0,1:T(8,128)} %copy-done.54, ...), dimensions={1} | concatenate | bytes 3219456
  1291.9 49.0 %concatenate.8 = f32[262,1536]{1,0:T(8,128)} concatenate(f32[6,1536]{1,0:T(8,128)S(1)} %collective-permute-done.31, f32[8,1536]{1,0:T(8,128)} %collective-permute-done.30, f32[8,1536]{1,0:T(8,128)} %collective-permute-done.29, f32[8,1536]{1,0:T(8,128)} %collective-permute-done.28, f32[8,1536]{1,0:T(8,128)} %collective-permute-done.27, f32[8,1536]{1,0:T(8,128)} %collective-permute-done.26, ...), dimensions={0} | concatenate | bytes 3219456
  1349.2 637.5 %all-reduce.6 = (f32[768]{0:T(1024)}, f32[768]{0:T(1024)}, f32[2,384]{1,0:T(2,128)}, f32[768]{0:T(1024)}, f32[768]{0:T(1024)}, /*index=5*/f32[768]{0:T(1024)}, f32[1536]{0:T(1024)}, f32[768]{0:T(1024)}) all-reduce(f32[768]{0:T(1024)S(1)} %get-tuple-element.179, ...), channel_id=1, replica_groups=mesh['dp'=128,'mp'=2] {'dp'}, use_global_device_ids=true, to_apply=%region_20.21 | all-reduce | flops 6912 | bytes 55296 | tf_op jit(solution)/shard_map/psum | solution.py:197
  1993.1 74.1 %all-reduce.19.cloned.1.call-done = (f32[768,3,384]{2,0,1:T(8,128)}, f32[384,768]{0,1:T(8,128)}) async-done(((f32[768,3,384]{2,0,1:T(8,128)}, f32[384,768]{0,1:T(8,128)}), (f32[768,3,384]{2,0,1:T(8,128)}, f32[384,768]{0,1:T(8,128)})) %all-reduce.19.cloned.1.call-update) | async-done | bytes 4718608
  (397 shorter events, 183.8 us)
Async XLA Ops:
  7.2 198.8 %all-gather.7.cloned.1.call-start = ((), (), s32[]{:S(2)}) async-start(), calls=%async_computation | async-start | bytes 2377728 | tf_op jit(solution)/shard_map/all_gather | solution.py:107
  8.0 240.4 %all-gather.9.cloned.1.call-start = ((), (), s32[]{:S(2)}) async-start(), calls=%async_computation.3 | async-start | bytes 3170304 | tf_op jit(solution)/shard_map/all_gather | solution.py:134
  8.7 356.8 %all-gather.11.cloned.1.call-start = ((), (), s32[]{:S(2)}) async-start(), calls=%async_computation.4 | async-start | bytes 3170304 | tf_op jit(solution)/shard_map/all_gather | solution.py:135
  9.5 453.0 %all-reduce.15.cloned.1.call-start = ((), (), s32[]{:S(2)}) async-start(), calls=%async_computation.1 | async-start | bytes 6291456 | tf_op jit(solution)/shard_map/psum | solution.py:130
  240.0 353.3 %all-reduce.17.cloned.1.call-start = ((), (), s32[]{:S(2)}) async-start(), calls=%async_computation.2 | async-start | bytes 6291456 | tf_op jit(solution)/shard_map/psum | solution.py:156
  494.7 851.5 %all-reduce.21.cloned.1.call-start = ((), (), s32[]{:S(2)}) async-start(), calls=%async_computation.6 | async-start | bytes 6291456 | tf_op jit(solution)/shard_map/psum | solution.py:141
  653.9 1413.3 %all-reduce.19.cloned.1.call-start = ((), (), s32[]{:S(2)}) async-start(), calls=%async_computation.5 | async-start | bytes 9437184
  1047.0 16.0 collective-permute-start.32
  1059.1 12.3 collective-permute-start.34
  1060.4 27.3 %collective-permute-start.35 = (f32[1536,8]{0,1:T(8,128)S(1)}, f32[1536,8]{0,1:T(8,128)S(1)}, u32[]{:S(2)}, u32[]{:S(2)}) collective-permute-start(f32[1536,8]{0,1:T(8,128)S(1)} %get-tuple-element.230), channel_id=1, source_target_pairs={{0,8},{2,10},{4,12},{6,14},{8,16},{10,18},{12,20},{14,22},{16,24},... | collective-permute-start | bytes 147464
  1061.7 30.3 %collective-permute-start.36 = (f32[1536,8]{0,1:T(8,128)S(1)}, f32[1536,8]{0,1:T(8,128)S(1)}, u32[]{:S(2)}, u32[]{:S(2)}) collective-permute-start(f32[1536,8]{0,1:T(8,128)S(1)} %get-tuple-element.230), channel_id=1, source_target_pairs={{0,10},{2,12},{4,14},{6,16},{8,18},{10,20},{12,22},{14,24},{16,26}... | collective-permute-start | bytes 147464
  1063.0 30.7 %collective-permute-start.37 = (f32[1536,8]{0,1:T(8,128)S(1)}, f32[1536,8]{0,1:T(8,128)S(1)}, u32[]{:S(2)}, u32[]{:S(2)}) collective-permute-start(f32[1536,8]{0,1:T(8,128)S(1)} %get-tuple-element.230), channel_id=1, source_target_pairs={{0,12},{2,14},{4,16},{6,18},{8,20},{10,22},{12,24},{14,26},{16,28}... | collective-permute-start | bytes 147464
  1064.3 34.9 %collective-permute-start.38 = (f32[1536,8]{0,1:T(8,128)S(1)}, f32[1536,8]{0,1:T(8,128)S(1)}, u32[]{:S(2)}, u32[]{:S(2)}) collective-permute-start(f32[1536,8]{0,1:T(8,128)S(1)} %get-tuple-element.230), channel_id=1, source_target_pairs={{0,14},{2,16},{4,18},{6,20},{8,22},{10,24},{12,26},{14,28},{16,30}... | collective-permute-start | bytes 147464
  1071.3 33.1 %collective-permute-start.39 = (f32[1536,8]{0,1:T(8,128)S(1)}, f32[1536,8]{0,1:T(8,128)S(1)}, u32[]{:S(2)}, u32[]{:S(2)}) collective-permute-start(f32[1536,8]{0,1:T(8,128)S(1)} %get-tuple-element.230), channel_id=1, source_target_pairs={{0,16},{2,18},{4,20},{6,22},{8,24},{10,26},{12,28},{14,30},{16,32}... | collective-permute-start | bytes 147464
  1087.7 18.3 collective-permute-start.40
  1092.0 20.0 collective-permute-start.41
  1093.7 19.7 collective-permute-start.42
  1099.2 15.6 collective-permute-start.43
  1104.4 16.6 collective-permute-start.44
  1106.0 17.2 collective-permute-start.45
  1112.1 12.5 collective-permute-start.46
  1113.4 12.5 collective-permute-start.47
  1114.8 14.3 collective-permute-start.48
  1140.4 12.6 collective-permute-start.59
  1142.1 16.8 collective-permute-start.60
  1144.4 15.8 collective-permute-start.61
  1146.1 15.5 collective-permute-start.62
  1148.8 17.8 collective-permute-start
  1153.0 17.9 collective-permute-start.1
  1159.0 13.2 collective-permute-start.10
  1160.3 13.5 collective-permute-start.11
  1161.6 14.9 collective-permute-start.12
  1166.6 13.0 collective-permute-start.13
  1173.8 12.5 collective-permute-start.16
  1176.5 13.8 collective-permute-start.17
  1179.6 12.6 collective-permute-start.18
  1180.9 13.2 collective-permute-start.19
  1182.3 13.8 collective-permute-start.2
  1186.3 13.4 collective-permute-start.20
  1207.3 13.9 collective-permute-start.29
  1209.2 15.1 collective-permute-start.3
  1211.2 16.4 collective-permute-start.30
  1213.1 23.0 %collective-permute-start.4 = (f32[8,1536]{1,0:T(8,128)S(1)}, f32[8,1536]{1,0:T(8,128)}, u32[]{:S(2)}, u32[]{:S(2)}) collective-permute-start(f32[8,1536]{1,0:T(8,128)S(1)} %get-tuple-element.229), channel_id=1, source_target_pairs={{0,10},{2,12},{4,14},{6,16},{8,18},{10,20},{12,22},{14,24},{16,26}... | collective-permute-start | bytes 147464
  1217.2 74.6 %collective-permute-start.5 = (f32[8,1536]{1,0:T(8,128)S(1)}, f32[8,1536]{1,0:T(8,128)}, u32[]{:S(2)}, u32[]{:S(2)}) collective-permute-start(f32[8,1536]{1,0:T(8,128)S(1)} %get-tuple-element.229), channel_id=1, source_target_pairs={{0,12},{2,14},{4,16},{6,18},{8,20},{10,22},{12,24},{14,26},{16,28}... | collective-permute-start | bytes 147464
  1221.2 70.6 %collective-permute-start.6 = (f32[8,1536]{1,0:T(8,128)S(1)}, f32[8,1536]{1,0:T(8,128)}, u32[]{:S(2)}, u32[]{:S(2)}) collective-permute-start(f32[8,1536]{1,0:T(8,128)S(1)} %get-tuple-element.229), channel_id=1, source_target_pairs={{0,14},{2,16},{4,18},{6,20},{8,22},{10,24},{12,26},{14,28},{16,30}... | collective-permute-start | bytes 147464
  1224.3 67.5 %collective-permute-start.7 = (f32[8,1536]{1,0:T(8,128)S(1)}, f32[8,1536]{1,0:T(8,128)}, u32[]{:S(2)}, u32[]{:S(2)}) collective-permute-start(f32[8,1536]{1,0:T(8,128)S(1)} %get-tuple-element.229), channel_id=1, source_target_pairs={{0,16},{2,18},{4,20},{6,22},{8,24},{10,26},{12,28},{14,30},{16,32}... | collective-permute-start | bytes 147464
  1227.6 64.2 %collective-permute-start.8 = (f32[8,1536]{1,0:T(8,128)S(1)}, f32[8,1536]{1,0:T(8,128)}, u32[]{:S(2)}, u32[]{:S(2)}) collective-permute-start(f32[8,1536]{1,0:T(8,128)S(1)} %get-tuple-element.229), channel_id=1, source_target_pairs={{0,18},{2,20},{4,22},{6,24},{8,26},{10,28},{12,30},{14,32},{16,34}... | collective-permute-start | bytes 147464
  1236.5 55.4 %collective-permute-start.9 = (f32[8,1536]{1,0:T(8,128)S(1)}, f32[8,1536]{1,0:T(8,128)}, u32[]{:S(2)}, u32[]{:S(2)}) collective-permute-start(f32[8,1536]{1,0:T(8,128)S(1)} %get-tuple-element.229), channel_id=1, source_target_pairs={{0,20},{2,22},{4,24},{6,26},{8,28},{10,30},{12,32},{14,34},{16,36}... | collective-permute-start | bytes 147464
  (117 other events, 5908.9 us)
Sparse Core Ops, SparseCore 0:
  11.7 119.9 all-gather.6
  135.5 112.8 all-gather.8
  252.2 113.2 all-gather.10
  368.6 93.7 all-reduce.14
  494.8 98.5 all-reduce.16
  654.1 133.3 all-reduce.20
  790.4 1276.8 all-reduce.18
where the time goes:
time: 2090 us; the launch traced here: 2080 us
  blocking collectives  1200 us (57%)
  waiting for transfers between devices  375 us (18%)
  starting transfers between devices  190 us (9%)
  local copies, waits for them, and re-layouts  161 us (8%)
  matrix products  85.9 us (4%)
  other arithmetic  47.4 us (2%)
    psum x1, blocking collectives, on_device(): lax.psum((jnp.sum(grad_normed_one * scaled_one, axis=0), jnp.sum(grad_nor...  638 us
    unnamed x1, blocking collectives  373 us
    unnamed x65, starting transfers between devices  190 us
    all_gather x1, blocking collectives, on_device(): lax.all_gather(out_weight, 'dp', axis=1, tiled=True)  189 us
    unnamed x188, local copies, waits for them, and re-layouts  125 us
    all_gather x1, waiting for transfers between devices, on_device(): lax.all_gather(fc2_weight, 'dp', axis=1, tiled=True)  112 us
    psum x1, waiting for transfers between devices, on_device(): mid = feature_rows + lax.psum(branch_part, 'mp') + out_bias  91.8 us
    psum x1, waiting for transfers between devices, on_device(): grad_normed_two = lax.psum(normed_two_part, 'mp')  86.4 us
  transfers between devices with their start and end apart: 71, of which 5 were waited for; matrix products, arithmetic and copies ran while one was open for 27% of the time, Pallas kernels for 0%

commit v1 on v0

v1 whole, which is shorter than its diff:
```python
import jax
import jax.numpy as jnp
from jax import lax
from jax.experimental import pallas as pl
from jax.experimental.pallas import tpu as pltpu
from jax.sharding import Mesh, PartitionSpec as P

F32 = jnp.float32
BF16 = jnp.bfloat16
EPS = 1e-06
MASKED = -1e30
VMEM = pl.BlockSpec(memory_space=pltpu.VMEM)
SMEM = pl.BlockSpec(memory_space=pltpu.SMEM)


def dot_nn(a, b):
    return lax.dot_general(a, b, (((1,), (0,)), ((), ())), preferred_element_type=F32)


def dot_nt(a, b):
    return lax.dot_general(a, b, (((1,), (1,)), ((), ())), preferred_element_type=F32)


def normalize(values):
    row_mean = jnp.mean(values, axis=-1, keepdims=True)
    centred = values - row_mean
    inv_std = lax.rsqrt(jnp.mean(centred * centred, axis=-1, keepdims=True) + EPS)
    return centred * inv_std, inv_std


def norm_back(grad_normed, gain_row, scaled, inv_std):
    grad_scaled = grad_normed * gain_row
    first_mean = jnp.mean(grad_scaled, axis=-1, keepdims=True)
    second_mean = jnp.mean(grad_scaled * scaled, axis=-1, keepdims=True)
    return inv_std * (grad_scaled - first_mean - scaled * second_mean)


def head_lanes(values, head):
    lane = lax.broadcasted_iota(jnp.int32, values.shape, 1)
    return jnp.where((lane >= 64) == (head == 1), values, jnp.zeros_like(values))


def pick_lanes(first, second):
    lane = lax.broadcasted_iota(jnp.int32, first.shape, 1)
    return jnp.where(lane < 64, first, second)


def columns(ref, head_pairs, lead=()):
    return jnp.concatenate([ref[(*lead, p)] for p in head_pairs], axis=1)


def forward_attention(count_ref, x_ref, g1_ref, b1_ref, w_ref, qb_ref, vb_ref, ob_ref, g2_ref, b2_ref,
                      n1_ref, qkv_ref, ctx_ref, lse_ref, mid_ref, n2_ref):
    rows = x_ref.shape[0]
    pairs = w_ref.shape[1]
    count = count_ref[0]
    scaled, _ = normalize(x_ref[...].astype(F32))
    n1_ref[...] = (scaled * g1_ref[...] + b1_ref[...]).astype(BF16)
    valid = lax.broadcasted_iota(jnp.int32, (rows, rows), 0) < count

    def pair(p, _):
        weight = jnp.concatenate([w_ref[0, p], w_ref[2, p], w_ref[1, p]], axis=1)
        projected = dot_nn(n1_ref[...], weight)
        query = (projected[:, :128] + qb_ref[pl.ds(p, 1), :]).astype(BF16) * BF16(0.125)
        key = projected[:, 128:256].astype(BF16)
        value = (projected[:, 256:] + vb_ref[pl.ds(p, 1), :]).astype(BF16)
        qkv_ref[0, p] = query
        qkv_ref[1, p] = key
        qkv_ref[2, p] = value
        value_t = value.T
        parts = []
        for head in range(2):
            scores = jnp.where(valid, dot_nt(head_lanes(key, head), query), MASKED)
            top = jnp.max(scores, axis=0, keepdims=True)
            shifted = jnp.exp(scores - top)
            total = jnp.sum(shifted, axis=0, keepdims=True)
            prob = shifted * (1.0 / total)
            parts.append(dot_nn(value_t[64 * head : 64 * head + 64], prob.astype(BF16)))
            lse_ref[p, pl.ds(head, 1), :] = top + jnp.log(total)
        ctx_ref[p] = jnp.concatenate(parts, axis=0).T.astype(BF16)
        return 0

    lax.fori_loop(0, pairs, pair, 0)
    context = columns(ctx_ref, range(pairs))
    for j in range(3):
        cols = slice(256 * j, 256 * j + 256)
        out = jnp.concatenate([w_ref[3, p, cols, :] for p in range(pairs)], axis=1)
        mid_ref[:, cols] = x_ref[:, cols].astype(F32) + dot_nt(context, out) + ob_ref[:, cols]
    scaled, _ = normalize(mid_ref[...])
    n2_ref[...] = (scaled * g2_ref[...] + b2_ref[...]).astype(BF16)


def call_forward(count, x, g1, b1, w, qb, vb, ob, g2, b2):
    rows, width = x.shape
    pairs = w.shape[1]
    S = jax.ShapeDtypeStruct
    return pl.pallas_call(
        forward_attention,
        in_specs=[SMEM] + [VMEM] * 9,
        out_specs=[VMEM] * 6,
        out_shape=[S((rows, width), BF16), S((3, pairs, rows, 128), BF16), S((pairs, rows, 128), BF16),
                   S((pairs, 2, rows), F32), S((rows, width), F32), S((rows, width), BF16)],
        compiler_params=pltpu.CompilerParams(vmem_limit_bytes=50 << 20),
        cost_estimate=pl.CostEstimate(flops=6 * 10**9, bytes_accessed=16 << 20, transcendentals=3 << 20),
        name="attention_forward",
    )(count, x, g1, b1, w, qb, vb, ob, g2, b2)


def feed_forward(n2_ref, cot_ref, mid_ref, b2_ref, w_ref, b1_ref, lo_ref, gn2_ref, dw_ref, db_ref,
                 n2t_ref, cott_ref, acc_ref):
    step = pl.program_id(0)
    last = pl.num_programs(0) - 1

    @pl.when(step == 0)
    def _():
        n2t_ref[...] = n2_ref[...].T
        cott_ref[...] = cot_ref[...].T
        acc_ref[...] = jnp.zeros_like(acc_ref)
        gn2_ref[...] = jnp.zeros_like(gn2_ref)

    blocks, half = w_ref.shape[0], w_ref.shape[1] // 2
    first = jnp.concatenate([w_ref[b, i] for b in range(blocks) for i in range(half)], axis=1)
    second = jnp.concatenate([w_ref[b, half + i] for b in range(blocks) for i in range(half)], axis=1)
    hidden = dot_nn(n2_ref[...], first) + b1_ref[0]
    cdf = 0.5 * (1.0 + lax.erf(hidden * 0.7071067811865476))
    slope = cdf + hidden * (jnp.exp(-0.5 * hidden * hidden) * 0.3989422804014327)
    active = (hidden * cdf).astype(BF16)
    acc_ref[...] += dot_nt(active, second)
    grad_hidden = dot_nn(cot_ref[...], second) * slope
    db_ref[0] = jnp.sum(grad_hidden, axis=0, keepdims=True)
    grad_hidden = grad_hidden.astype(BF16)
    gn2_ref[...] += dot_nt(grad_hidden, first)
    fc2 = dot_nn(cott_ref[...], active).astype(BF16)
    fc1 = dot_nn(n2t_ref[...], grad_hidden).astype(BF16)
    for b in range(blocks):
        for i in range(half):
            at = 128 * (b * half + i)
            dw_ref[b, i] = fc1[:, at : at + 128]
            dw_ref[b, half + i] = fc2[:, at : at + 128]

    @pl.when(step == last)
    def _():
        lo_ref[...] = (mid_ref[...] + acc_ref[...] + b2_ref[...]).astype(BF16)


def call_feed_forward(n2, cot, mid, b2, w, b1):
    rows, width = n2.shape
    S = jax.ShapeDtypeStruct
    per = 2
    steps = w.shape[0] // per
    hidden = per * w.shape[1] // 2 * 128
    whole = pl.BlockSpec((rows, width), lambda i: (0, 0))
    block = pl.BlockSpec((per, *w.shape[1:]), lambda i: (i, 0, 0, 0))
    bias = pl.BlockSpec((1, 1, hidden), lambda i: (i, 0, 0))
    return pl.pallas_call(
        feed_forward,
        grid=(steps,),
        in_specs=[whole, whole, whole, pl.BlockSpec((1, width), lambda i: (0, 0)), block, bias],
        out_specs=[whole, whole, block, bias],
        out_shape=[S((rows, width), BF16), S((rows, width), F32), S(w.shape, BF16), S((steps, 1, hidden), F32)],
        scratch_shapes=[pltpu.VMEM((width, rows), BF16), pltpu.VMEM((width, rows), BF16), pltpu.VMEM((rows, width), F32)],
        compiler_params=pltpu.CompilerParams(vmem_limit_bytes=56 << 20),
        cost_estimate=pl.CostEstimate(flops=15 * 10**9, bytes_accessed=24 << 20, transcendentals=3 << 20),
        name="feed_forward",
    )(n2, cot, mid, b2, w, b1.reshape(steps, 1, hidden))


def backward_attention(count_ref, x_ref, g1_ref, w_ref, g2_ref, n1_ref, qkv_ref, ctx_ref, lse_ref, mid_ref, cot_ref, gn2_ref,
                       fg_ref, dw_ref, small_ref, qvb_ref, gb_ref, gbt_ref, n1t_ref, gm_ref):
    rows, width = x_ref.shape
    pairs = w_ref.shape[1]
    count = count_ref[0]
    scaled, inv = normalize(mid_ref[...])
    cot = cot_ref[...].astype(F32)
    gn2 = gn2_ref[...]
    grad_mid = cot + norm_back(gn2, g2_ref[...], scaled, inv)
    gm_ref[...] = grad_mid
    branch = grad_mid.astype(BF16)
    gb_ref[...] = branch
    gbt_ref[...] = branch.T
    n1t_ref[...] = n1_ref[...].T
    small_ref[2:3, :] = jnp.sum(branch.astype(F32), axis=0, keepdims=True)
    small_ref[3:4, :] = jnp.sum(gn2 * scaled, axis=0, keepdims=True)
    small_ref[4:5, :] = jnp.sum(gn2, axis=0, keepdims=True)
    small_ref[5:6, :] = jnp.sum(cot, axis=0, keepdims=True)
    valid = lax.broadcasted_iota(jnp.int32, (rows, rows), 0) < count
    fg_ref[...] = jnp.zeros_like(fg_ref)

    def pair(p, _):
        query, key, value = qkv_ref[0, p], qkv_ref[1, p], qkv_ref[2, p]
        grad_context = dot_nn(gb_ref[...], w_ref[3, p]).astype(BF16)
        dw_ref[3, p] = dot_nn(gbt_ref[...], ctx_ref[p]).astype(BF16)
        key_t = key.T
        grad_q, grad_k, grad_v = [], [], []
        for head in range(2):
            scores = jnp.where(valid, dot_nt(head_lanes(key, head), query), MASKED)
            prob = jnp.exp(scores - lse_ref[p, pl.ds(head, 1), :])
            grad_prob = dot_nt(head_lanes(value, head), grad_context)
            delta = jnp.sum(prob * grad_prob, axis=0, keepdims=True)
            grad_scores = (prob * (grad_prob - delta)).astype(BF16)
            grad_k.append(dot_nn(grad_scores, query))
            grad_v.append(dot_nn(prob.astype(BF16), grad_context))
            grad_q.append(dot_nn(key_t[64 * head : 64 * head + 64], grad_scores))
        grad_query = (jnp.concatenate(grad_q, axis=0).T * 0.125).astype(BF16)
        grad_key = pick_lanes(*grad_k).astype(BF16)
        grad_value = pick_lanes(*grad_v).astype(BF16)
        qvb_ref[0, pl.ds(p, 1), :] = jnp.sum(grad_query.astype(F32), axis=0, keepdims=True)
        qvb_ref[1, pl.ds(p, 1), :] = jnp.sum(grad_value.astype(F32), axis=0, keepdims=True)
        joined = jnp.concatenate([grad_query, grad_value, grad_key], axis=1)
        weight = jnp.concatenate([w_ref[0, p], w_ref[1, p], w_ref[2, p]], axis=1)
        fg_ref[...] += dot_nt(joined, weight)
        grads = dot_nn(n1t_ref[...], joined).astype(BF16)
        for i in range(3):
            dw_ref[i, p] = grads[:, 128 * i : 128 * i + 128]
        return 0

    lax.fori_loop(0, pairs, pair, 0)
    gn1 = fg_ref[...]
    scaled, inv = normalize(x_ref[...].astype(F32))
    small_ref[0:1, :] = jnp.sum(gn1 * scaled, axis=0, keepdims=True)
    small_ref[1:2, :] = jnp.sum(gn1, axis=0, keepdims=True)
    fg_ref[...] = gm_ref[...] + norm_back(gn1, g1_ref[...], scaled, inv)


def call_backward(count, x, g1, w, g2, n1, qkv, ctx, lse, mid, cot, gn2):
    rows, width = x.shape
    pairs = w.shape[1]
    S = jax.ShapeDtypeStruct
    return pl.pallas_call(
        backward_attention,
        in_specs=[SMEM] + [VMEM] * 11,
        out_specs=[VMEM] * 4,
        out_shape=[S((rows, width), F32), S(w.shape, BF16), S((6, width), F32), S((2, pairs, 128), F32)],
        scratch_shapes=[pltpu.VMEM((rows, width), BF16), pltpu.VMEM((width, rows), BF16), pltpu.VMEM((width, rows), BF16), pltpu.VMEM((rows, width), F32)],
        compiler_params=pltpu.CompilerParams(vmem_limit_bytes=56 << 20),
        cost_estimate=pl.CostEstimate(flops=14 * 10**9, bytes_accessed=24 << 20, transcendentals=3 << 20),
        name="attention_backward",
    )(count, x, g1, w, g2, n1, qkv, ctx, lse, mid, cot, gn2)


NAMES = ("z", "x", "yh", "core", "yl")
SIZES = (8, 4, 2, 2, 2)
DP = ("z", "x", "yh", "core")
Y = ("yh", "yl")
QUARTER = ("yh", "core")


def swap(values, axis, n, k):
    return lax.ppermute(values, axis, [(i, i ^ k) for i in range(n)])


def pick(values, index, axis=0):
    return lax.dynamic_index_in_dim(values, index, axis, keepdims=False)


def in_order(parts, index, axis):
    bit = 1
    while bit < len(parts):
        flip = (index & bit) != 0
        parts = [jnp.where(flip, parts[k ^ bit], parts[k]) for k in range(len(parts))]
        bit *= 2
    return jnp.stack(parts, axis=axis)


def gather(values, axis, n, index, place):
    return in_order([values] + [swap(values, axis, n, k) for k in range(1, n)], index, place)


def scatter_sum(values, axis, n, index, place):
    total = pick(values, index, place).astype(F32)
    for k in range(1, n):
        total = total + swap(pick(values, index ^ k, place), axis, n, k).astype(F32)
    return total.astype(BF16)


def gather_weights(packed, at):
    c = packed.shape[1]
    own = [pick(packed, at["q"])] + [swap(pick(packed, at["q"] ^ k), QUARTER, 4, k) for k in (1, 2, 3)]
    rows = in_order(own, at["q"], 1).reshape(c, 24, 128)
    rows = gather(rows, "z", 8, at["z"], 1)
    low, high = rows[:, :4], rows[:, 4:]
    low = gather(low, "x", 4, at["x"], 2).reshape(c, 384, 128)
    high = gather(high, Y, 4, at["y"], 0)
    low = gather(low, Y, 4, at["y"], 0)
    high = gather(high, "x", 4, at["x"], 3).reshape(4, c, 384, 128)
    both = jnp.concatenate([low, high], axis=2)
    return gather(both, "core", 2, at["core"], 0)


def scatter_grads(grads, at):
    c = grads.shape[2]
    total = scatter_sum(grads, "core", 2, at["core"], 0)
    low = total[:, :, :384]
    high = total[:, :, 384:].reshape(4, c, 4, 4, 24, 128)
    low = scatter_sum(low, Y, 4, at["y"], 0).reshape(c, 4, 4, 24, 128)
    high = scatter_sum(high, "x", 4, at["x"], 3)
    low = scatter_sum(low, "x", 4, at["x"], 2)
    high = scatter_sum(high, Y, 4, at["y"], 0)
    rows = scatter_sum(jnp.concatenate([low, high], axis=1), "z", 8, at["z"], 1)
    rows = rows.reshape(c, 4, 6, 128)
    own = [pick(rows, at["q"], 1)] + [swap(pick(rows, at["q"] ^ k, 1), QUARTER, 4, k) for k in (1, 2, 3)]
    return in_order(own, at["q"], 0).astype(F32)


def sum_everywhere(values):
    for axis, n in (("core", 2), ("yl", 2), ("yh", 2), ("x", 4), ("z", 8)):
        k = 1
        while k < n:
            values = values + swap(values, axis, n, k)
            k *= 2
    return values


def share(mine, at):
    other = swap(mine, "yl", 2, 1)
    mine = mine.astype(other.dtype)
    return jnp.stack([jnp.where(at["yl"] == 0, mine, other), jnp.where(at["yl"] == 0, other, mine)])


def on_device(
    features, patch_counts, ln1_gain, ln1_bias, query_key_value_weight, qv_bias, out_weight, out_bias,
    ln2_gain, ln2_bias, fc1_weight, fc1_bias, fc2_weight, fc2_bias, cotangent,
):
    at = {name: lax.axis_index(name) for name in NAMES}
    at["y"] = at["yh"] * 2 + at["yl"]
    at["q"] = at["yh"] * 2 + at["core"]
    row = lambda v: v.reshape(1, -1)

    attention_packed = jnp.concatenate(
        [
            query_key_value_weight.reshape(6, 3, 3, 128).transpose(1, 2, 0, 3),
            out_weight.reshape(1, 3, 128, 6).transpose(0, 1, 3, 2),
        ]
    )
    fc_packed = jnp.concatenate(
        [
            fc1_weight.reshape(6, 4, 3, 128).transpose(1, 2, 0, 3),
            fc2_weight.reshape(4, 3, 128, 6).transpose(0, 1, 3, 2),
        ],
        axis=1,
    )
    biases = jnp.concatenate([qv_bias.reshape(-1), fc1_bias]).reshape(18, 128)
    biases = gather(biases, "yl", 2, at["yl"], 0)
    query_bias = biases[:, 0:3].reshape(6, 128)
    value_bias = biases[:, 3:6].reshape(6, 128)
    hidden_bias = biases[:, 6:].reshape(2, 2, 2, 384).transpose(2, 1, 0, 3).reshape(-1)

    attention = gather_weights(attention_packed, at).reshape(4, 6, 768, 128)
    fc = gather_weights(fc_packed, at).reshape(8, 6, 768, 128)

    item = pick(features, at["yl"])
    cot = pick(cotangent, at["yl"])
    count = pick(patch_counts, at["yl"]).reshape(1)

    n1, qkv, context, log_total, mid, n2 = call_forward(
        count, item, row(ln1_gain), row(ln1_bias), attention, query_bias, value_bias, row(out_bias), row(ln2_gain), row(ln2_bias)
    )
    out_rows, gn2, fc_grads, hidden_sums = call_feed_forward(n2, cot, mid, row(fc2_bias), fc, hidden_bias)
    layer_out = share(out_rows, at)
    fc_own = scatter_grads(fc_grads.reshape(2, 4, 6, 768, 128), at)
    fg, attention_grads, sums, qv_sums = call_backward(
        count, item, row(ln1_gain), attention, row(ln2_gain), n1, qkv, context, log_total, mid, cot, gn2
    )
    attention_own = scatter_grads(attention_grads.reshape(2, 4, 3, 768, 128), at)

    other = swap(fg.astype(BF16), "yl", 2, 1).astype(F32)
    first = at["yl"] == 0
    features_grad = jnp.stack([jnp.where(first, fg, other), jnp.where(first, other, fg)])

    small = jnp.concatenate([sums.reshape(36, 128), qv_sums.reshape(12, 128), hidden_sums.reshape(24, 128)])
    small = sum_everywhere(small)
    sums = small[:36].reshape(6, 768)
    qv_grad = pick(small[36:48].reshape(2, 2, 384), at["yl"], 1)
    hidden_grad = pick(small[48:].reshape(2, 2, 2, 384), at["yl"], 2).transpose(1, 0, 2).reshape(1536)

    qkv_grad = attention_own[:3].transpose(2, 0, 1, 3).reshape(6, 3, 384)
    out_grad = attention_own[3].transpose(0, 2, 1).reshape(384, 6)
    fc1_grad = fc_own[:, :3].transpose(2, 0, 1, 3).reshape(6, 1536)
    fc2_grad = fc_own[:, 3:].transpose(0, 1, 3, 2).reshape(1536, 6)
    return (
        layer_out, features_grad, sums[0], sums[1], qkv_grad, qv_grad, out_grad, sums[2], sums[3], sums[4],
        fc1_grad, hidden_grad, fc2_grad, sums[5],
    )


def solution(mesh):
    five = Mesh(mesh.devices.reshape(SIZES), NAMES)
    return jax.shard_map(
        on_device,
        mesh=five,
        in_specs=(
            P(DP, None, None), P(DP), P(), P(), P(DP, None, "yl"), P(None, "yl"), P("yl", DP), P(),
            P(), P(), P(DP, "yl"), P("yl"), P("yl", DP), P(), P(DP, None, None),
        ),
        out_specs=(
            P(DP, None, None), P(DP, None, None), P(), P(), P(DP, None, "yl"), P(None, "yl"), P("yl", DP), P(),
            P(), P(), P(DP, "yl"), P("yl"), P("yl", DP), P(),
        ),
        check_vma=False,
    )
```

time: 2090 us -> 469 us (0.22)
  blocking collectives: 1200 us -> 0 us
  waiting for transfers between devices: 375 us -> 139 us
  local copies, waits for them, and re-layouts: 161 us -> 21.9 us
  matrix products: 85.9 us -> 0 us
  Pallas kernels: 0 us -> 69 us
    psum x1 -> x0, blocking collectives: 638 us -> none  [on_device(): lax.psum((jnp.sum(grad_normed_one * scaled_one, axis=0), jnp.sum(grad_nor...]
    unnamed x1 -> x0, blocking collectives: 373 us -> none
    unnamed x65 -> x0, starting transfers between devices: 190 us -> none
    all_gather x1 -> x0, blocking collectives: 189 us -> none  [on_device(): lax.all_gather(out_weight, 'dp', axis=1, tiled=True)]
    psum x3 -> x0, waiting for transfers between devices: 178 us -> none  [the longest x1 91.8 us: on_device(): mid = feature_rows + lax.psum(branch_part, 'mp') + out_bias]
    ppermute x0 -> x103, starting transfers between devices: none -> 178 us  [swap(): return lax.ppermute(values, axis, [(i, i ^ k) for i in range(n)])]
    ppermute x0 -> x103, waiting for transfers between devices: none -> 139 us  [swap(): return lax.ppermute(values, axis, [(i, i ^ k) for i in range(n)])]
    unnamed x188 -> x77, local copies, waits for them, and re-layouts: 125 us -> 1.39 us
  transfers between devices with their start and end apart: 71 -> 103, of which waited for: 5 -> 30; matrix products, arithmetic and copies ran while one was open for 27% -> 11% of each run, Pallas kernels for 0% -> 4%
where the time goes in v1:
time: 469 us; the launch traced here: 460 us
  starting transfers between devices  178 us (38%)
  waiting for transfers between devices  139 us (30%)
  Pallas kernels  69 us (15%)
  other arithmetic  49.6 us (11%)
  local copies, waits for them, and re-layouts  21.9 us (5%)
    ppermute x103, starting transfers between devices, swap(): return lax.ppermute(values, axis, [(i, i ^ k) for i in range(n)])  178 us
    ppermute x103, waiting for transfers between devices, swap(): return lax.ppermute(values, axis, [(i, i ^ k) for i in range(n)])  139 us
    pallas_call x1, Pallas kernels, call_backward(): pl.pallas_call(backward_attention, in_specs=[SMEM] + [VMEM] * 11, out_spe...  30.3 us
    another operation x41, other arithmetic, in_order(): return jnp.stack(parts, axis=axis)  24.5 us
    pallas_call x1, Pallas kernels, call_feed_forward(): pl.pallas_call(feed_forward, grid=(steps,), in_specs=[whole, whole, whole...  21.8 us
    pallas_call x1, Pallas kernels, call_forward(): pl.pallas_call(forward_attention, in_specs=[SMEM] + [VMEM] * 9, out_specs...  16.9 us
    squeeze x13, local copies, waits for them, and re-layouts, pick(): return lax.dynamic_index_in_dim(values, index, axis, keepdims=False)  12.8 us
    convert_element_type x12, other arithmetic, scatter_sum(): return total.astype(BF16)  9.56 us
  transfers between devices with their start and end apart: 103, of which 30 were waited for; matrix products, arithmetic and copies ran while one was open for 11% of the time, Pallas kernels for 4%

profile of v1, /device:TPU:1, one launch (start us, length us, event | category | flops | bytes accessed | tf_op | source)
XLA Modules:
  0.0 460.0 jit_solution(12819693813257853787)
XLA Ops:
  2.2 4.4 collective-permute-start
  13.9 4.4 collective-permute-start.3
  18.8 3.5 collective-permute-start.5
  31.2 2.9 collective-permute-start.29
  44.0 3.0 collective-permute-start.16
  65.7 20.1 %collective-permute-done.43 = bf16[4,6,4,24,128]{4,3,1,2,0:T(8,128)(2,1)S(1)} collective-permute-done((bf16[4,6,4,24,128]{4,3,1,2,0:T(8,128)(2,1)S(1)}, bf16[4,6,4,24,128]{4,3,1,2,0:T(8,128)(2,1)S(1)}, u32[]{:S(2)}, u32[]{:S(2)}) %collective-permute-start.43) | collective-permute-done | bytes 589856 | tf_op jit(solution)/shard_map/ppermute | solution.py:249
  85.7 3.4 collective-permute-start.37
  92.7 21.1 %collective-permute-done.37 = bf16[6,384,128]{2,1,0:T(8,128)(2,1)S(1)} collective-permute-done((bf16[6,384,128]{2,1,0:T(8,128)(2,1)S(1)}, bf16[6,384,128]{2,1,0:T(8,128)(2,1)S(1)}, u32[]{:S(2)}, u32[]{:S(2)}) %collective-permute-start.37) | collective-permute-done | bytes 589856 | tf_op jit(solution)/shard_map/ppermute | solution.py:249
  113.8 3.9 collective-permute-start.19
  118.6 3.1 pad_maximum_fusion.2
  121.7 8.7 %collective-permute-done.19 = bf16[4,3,4,24,128]{4,3,1,2,0:T(8,128)(2,1)S(1)} collective-permute-done((bf16[4,3,4,24,128]{4,3,1,2,0:T(8,128)(2,1)S(1)}, bf16[4,3,4,24,128]{4,3,1,2,0:T(8,128)(2,1)S(1)}, u32[]{:S(2)}, u32[]{:S(2)}) %collective-permute-start.19) | collective-permute-done | bytes 294944 | tf_op jit(solution)/shard_map/ppermute | solution.py:249
  132.8 4.5 collective-permute-done.15
  147.6 3.3 select_bitcast_fusion.3
  153.6 16.9 %attention_forward.1 = (bf16[512,768]{1,0:T(8,128)(2,1)S(1)}, bf16[3,6,512,128]{3,2,1,0:T(8,128)(2,1)}, bf16[6,512,128]{2,1,0:T(8,128)(2,1)S(1)}, f32[6,2,512]{2...) custom-call(s32[1]{0:T(128)} %dynamic_slice.239.count_ref, ...), custom_call_target="tpu_custom_call" | custom-call | flops 6000000000 | bytes 16777216 | tf_op jit(solution)/shard_map/attention_forward/pallas_call | solution.py:97
  170.6 8.1 %select_bitcast_fusion.1 = (bf16[1,4,6,768,128]{4,3,2,1,0:T(8,128)(2,1)}, bf16[1,4,6,768,128]{4,3,2,1,0:T(8,128)(2,1)}) fusion(bf16[4,6,768,128]{3,2,1,0:T(8,128)(2,1)} %collective-permute-done.46, pred[]{:T(512)S(6)} %ne.22, bf16[4,6,384,128]{3,2,1,0:T(8,128)(2,1)S(1)} %bitcast.417, bf16[1,6,384,128]{3,2,1,0:T(8,128)(2,1)S(1)} %copy-done.17, ...), kind=kLoop, calls=%fused_computation.9 | loop fusion | flops 28311552 | bytes 18874368 | tf_op jit(solution)/shard_map/stack | solution.py:262
  178.7 8.2 %pad_maximum_fusion = bf16[2,4,6,768,128]{4,3,2,1,0:T(8,128)(2,1)} fusion(bf16[1,4,6,768,128]{4,3,2,1,0:T(8,128)(2,1)} %get-tuple-element.79, bf16[1,4,6,768,128]{4,3,2,1,0:T(8,128)(2,1)} %get-tuple-element.78), kind=kLoop, calls=%fused_computation | loop fusion | flops 4718592 | bytes 18874368 | tf_op jit(solution)/shard_map/stack | solution.py:262
  186.9 21.8 %feed_forward.1 = (bf16[512,768]{1,0:T(8,128)(2,1)}, f32[512,768]{1,0:T(8,128)}, bf16[8,6,768,128]{3,2,1,0:T(8,128)(2,1)}, f32[4,1,768]{2,1,0:T(1,128)}) custom-call(bf16[512,768]{1,0:T(8,128)(2,1)} %copy-done.5, bf16[512,768]{1,0:T(8,128)(2,1)} %get-tuple-element.214.cot_ref, f32[512,768]{1,0:T(8,128)} %get-tuple-element.29.mid_ref, ...), custom_call_target="tpu_custom_call" | custom-call | flops 15000000512 | bytes 25165824 | tf_op jit(solution)/shard_map/feed_forward/pallas_call | solution.py:155
  208.7 30.3 %attention_backward.1 = (f32[512,768]{1,0:T(8,128)}, bf16[4,6,768,128]{3,2,1,0:T(8,128)(2,1)}, f32[6,768]{1,0:T(8,128)}, f32[2,6,128]{2,1,0:T(8,128)}) custom-call(s32[1]{0:T(128)} %dynamic_slice.239.count_ref, bf16[512,768]{1,0:T(8,128)(2,1)} %copy-done, f32[1,768]{1,0:T(1,128)} %copy-done.1, bf16[4,6,768,128]{3,2,1,0:T(8,128)(2,1)} %bitcast.430, ...), custom_call_target="tpu_custom_call" | custom-call | flops 14000000000 | bytes 25165824 | tf_op jit(solution)/shard_map/attention_backward/pallas_call | solution.py:229
  239.1 3.2 dynamic-slice_bitcast_fusion.1
  242.6 5.1 %dynamic-slice_bitcast_fusion = bf16[4,6,768,128]{3,2,1,0:T(8,128)(2,1)} fusion(bf16[2,4,6,768,128]{4,3,2,1,0:T(8,128)(2,1)} %bitcast.421, s32[]{:T(128)S(6)} %select_n.1019), kind=kLoop, calls=%fused_computation.7 | loop fusion | bytes 9437188 | tf_op jit(solution)/shard_map/jit(dynamic_index_in_dim)/squeeze | solution.py:253
  249.9 3.3 collective-permute-done.49
  255.0 13.3 %collective-permute-done.50 = f32[72,128]{1,0:T(8,128)S(1)} collective-permute-done((f32[72,128]{1,0:T(8,128)S(1)}, f32[72,128]{1,0:T(8,128)S(1)}, u32[]{:S(2)}, u32[]{:S(2)}) %collective-permute-start.50) | collective-permute-done | bytes 36896 | tf_op jit(solution)/shard_map/ppermute | solution.py:249
  268.2 4.6 %collective-permute-start.51 = (f32[72,128]{1,0:T(8,128)S(1)}, f32[72,128]{1,0:T(8,128)S(1)}, u32[]{:S(2)}, u32[]{:S(2)}) collective-permute-start(f32[72,128]{1,0:T(8,128)S(1)} %add.297), channel_id=1, source_target_pairs={{0,4},{4,0},{1,5},{5,1},{2,6},{6,2},{3,7},{7,3},{8,12},{12,8},{9,1... | collective-permute-start | bytes 110600 | tf_op jit(solution)/shard_map/ppermute | solution.py:249
  274.2 2.8 collective-permute-done.52
  277.1 3.1 collective-permute-start.53
  281.5 3.1 collective-permute-done.54
  284.8 3.5 collective-permute-done.55
  288.3 3.3 collective-permute-start.56
  292.5 3.3 collective-permute-done.56
  300.1 4.4 collective-permute-done.48
  305.9 3.2 fusion.1
  315.9 3.2 collective-permute-start.65
  321.5 3.7 collective-permute-start.62
  327.0 2.9 collective-permute-done.66
  341.4 3.4 collective-permute-start.73
  345.8 3.8 fusion
  350.0 3.5 collective-permute-start.75
  357.4 14.8 %collective-permute-start.77 = (bf16[3,6,128]{2,1,0:T(8,128)(2,1)S(1)}, bf16[3,6,128]{2,1,0:T(8,128)(2,1)S(1)}, u32[]{:S(2)}, u32[]{:S(2)}) collective-permute-start(bf16[3,6,128]{2,1,0:T(8,128)(2,1)S(1)} %get-tuple-element.203), channel_id=1, source_target_pairs={{0,6},{2,4},{4,2},{6,0},{1,7},{3,5},{5,3},{7,1},{8,14},{10,12},{12... | collective-permute-start | bytes 13832 | tf_op jit(solution)/shard_map/ppermute | solution.py:249
  377.9 5.6 %collective-permute-done.77 = bf16[3,6,128]{2,1,0:T(8,128)(2,1)S(1)} collective-permute-done((bf16[3,6,128]{2,1,0:T(8,128)(2,1)S(1)}, bf16[3,6,128]{2,1,0:T(8,128)(2,1)S(1)}, u32[]{:S(2)}, u32[]{:S(2)}) %collective-permute-start.77) | collective-permute-done | bytes 4640 | tf_op jit(solution)/shard_map/ppermute | solution.py:249
  383.9 5.7 %collective-permute-done.78 = bf16[3,6,128]{2,1,0:T(8,128)(2,1)S(1)} collective-permute-done((bf16[3,6,128]{2,1,0:T(8,128)(2,1)S(1)}, bf16[3,6,128]{2,1,0:T(8,128)(2,1)S(1)}, u32[]{:S(2)}, u32[]{:S(2)}) %collective-permute-start.78) | collective-permute-done | bytes 4640 | tf_op jit(solution)/shard_map/ppermute | solution.py:249
  390.3 3.1 collective-permute-start.89
  393.4 9.0 %collective-permute-done.83 = bf16[6,384,128]{2,1,0:T(8,128)(2,1)S(1)} collective-permute-done((bf16[6,384,128]{2,1,0:T(8,128)(2,1)}, bf16[6,384,128]{2,1,0:T(8,128)(2,1)S(1)}, u32[]{:S(2)}, u32[]{:S(2)}) %collective-permute-start.83) | collective-permute-done | bytes 589856 | tf_op jit(solution)/shard_map/ppermute | solution.py:249
  404.7 3.4 collective-permute-start.86
  408.1 4.6 %collective-permute-done.88 = bf16[4,6,4,24,128]{4,3,2,1,0:T(8,128)(2,1)S(1)} collective-permute-done((bf16[4,6,4,24,128]{4,3,2,1,0:T(8,128)(2,1)S(1)}, bf16[4,6,4,24,128]{4,3,2,1,0:T(8,128)(2,1)S(1)}, u32[]{:S(2)}, u32[]{:S(2)}) %collective-permute-start.88) | collective-permute-done | bytes 589856 | tf_op jit(solution)/shard_map/ppermute | solution.py:249
  415.5 5.6 %collective-permute-start.91 = (bf16[6,4,24,128]{3,2,1,0:T(8,128)(2,1)S(1)}, bf16[6,4,24,128]{3,2,1,0:T(8,128)(2,1)S(1)}, u32[]{:S(2)}, u32[]{:S(2)}) collective-permute-start(bf16[6,4,24,128]{3,2,1,0:T(8,128)(2,1)S(1)} %get-tuple-element.121), channel_id=1, source_target_pairs={{0,4},{1,5},{4,0},{5,1},{2,6},{3,7},{6,2},{7,3},{8,12},{9,13},{12,... | collective-permute-start | bytes 442376 | tf_op jit(solution)/shard_map/ppermute | solution.py:249
  430.4 3.2 collective-permute-start.96
  434.1 3.4 collective-permute-start.98
  441.6 13.4 %collective-permute-start.100 = (bf16[6,6,128]{2,1,0:T(8,128)(2,1)S(1)}, bf16[6,6,128]{2,1,0:T(8,128)(2,1)S(1)}, u32[]{:S(2)}, u32[]{:S(2)}) collective-permute-start(bf16[6,6,128]{2,1,0:T(8,128)(2,1)S(1)} %get-tuple-element.182), channel_id=1, source_target_pairs={{0,6},{2,4},{4,2},{6,0},{1,7},{3,5},{5,3},{7,1},{8,14},{10,12},{12... | collective-permute-start | bytes 27656 | tf_op jit(solution)/shard_map/ppermute | solution.py:249
  (376 shorter events, 137.7 us)
Async XLA Ops:
  2.2 11.2 %collective-permute-start = (bf16[3,6,128]{2,1,0:T(8,128)(2,1)S(1)}, bf16[3,6,128]{2,1,0:T(8,128)(2,1)S(1)}, u32[]{:S(2)}, u32[]{:S(2)}) collective-permute-start(bf16[3,6,128]{2,1,0:T(8,128)(2,1)S(1)} %get-tuple-element.212), channel_id=1, source_target_pairs={{0,6},{2,4},{4,2},{6,0},{1,7},{3,5},{5,3},{7,1},{8,14},{10,12},{12... | collective-permute-start | bytes 13832 | tf_op jit(solution)/shard_map/ppermute | solution.py:249
  11.6 10.7 %collective-permute-start.25 = (bf16[6,6,128]{2,1,0:T(8,128)(2,1)S(1)}, bf16[6,6,128]{2,1,0:T(8,128)(2,1)S(1)}, u32[]{:S(2)}, u32[]{:S(2)}) collective-permute-start(bf16[6,6,128]{2,1,0:T(8,128)(2,1)S(1)} %bitcast.456), channel_id=1, source_target_pairs={{0,4},{2,6},{4,0},{6,2},{1,5},{3,7},{5,1},{7,3},{8,12},{10,14},{12... | collective-permute-start | bytes 27656 | tf_op jit(solution)/shard_map/ppermute | solution.py:249
  13.4 10.7 %collective-permute-start.26 = (bf16[6,6,128]{2,1,0:T(8,128)(2,1)S(1)}, bf16[6,6,128]{2,1,0:T(8,128)(2,1)S(1)}, u32[]{:S(2)}, u32[]{:S(2)}) collective-permute-start(bf16[6,6,128]{2,1,0:T(8,128)(2,1)S(1)} %bitcast.458), channel_id=1, source_target_pairs={{0,2},{2,0},{4,6},{6,4},{1,3},{3,1},{5,7},{7,5},{8,10},{10,8},{12,... | collective-permute-start | bytes 27656 | tf_op jit(solution)/shard_map/ppermute | solution.py:249
  13.9 11.8 %collective-permute-start.3 = (bf16[3,24,128]{2,1,0:T(8,128)(2,1)S(1)}, bf16[3,24,128]{2,1,0:T(8,128)(2,1)S(1)}, u32[]{:S(2)}, u32[]{:S(2)}) collective-permute-start(bf16[3,24,128]{2,1,0:T(8,128)(2,1)S(1)} %reshape.195), channel_id=1, source_target_pairs={{0,224},{32,192},{64,160},{96,128},{128,96},{160,64},{192,32},{224... | collective-permute-start | bytes 55304 | tf_op jit(solution)/shard_map/ppermute | solution.py:249
  25.8 10.2 %collective-permute-start.9 = (bf16[3,24,128]{2,1,0:T(8,128)(2,1)S(1)}, bf16[3,24,128]{2,1,0:T(8,128)(2,1)S(1)}, u32[]{:S(2)}, u32[]{:S(2)}) collective-permute-start(bf16[3,24,128]{2,1,0:T(8,128)(2,1)S(1)} %reshape.195), channel_id=1, source_target_pairs={{0,32},{32,0},{64,96},{96,64},{128,160},{160,128},{192,224},{224,1... | collective-permute-start | bytes 55304 | tf_op jit(solution)/shard_map/ppermute | solution.py:249
  27.8 10.0 %collective-permute-start.27 = (bf16[6,24,128]{2,1,0:T(8,128)(2,1)S(1)}, bf16[6,24,128]{2,1,0:T(8,128)(2,1)S(1)}, u32[]{:S(2)}, u32[]{:S(2)}) collective-permute-start(bf16[6,24,128]{2,1,0:T(8,128)(2,1)S(1)} %reshape.209), channel_id=1, source_target_pairs={{0,224},{32,192},{64,160},{96,128},{128,96},{160,64},{192,32},{224... | collective-permute-start | bytes 110600 | tf_op jit(solution)/shard_map/ppermute | solution.py:249
  47.9 14.1 %collective-permute-start.34 = (bf16[6,4,24,128]{3,2,0,1:T(8,128)(2,1)S(1)}, bf16[6,4,24,128]{3,2,0,1:T(8,128)(2,1)S(1)}, u32[]{:S(2)}, u32[]{:S(2)}) collective-permute-start(bf16[6,4,24,128]{3,2,0,1:T(8,128)(2,1)S(1)} %pad_maximum_fusion.12), channel_id=1, source_target_pairs={{0,24},{8,16},{16,8},{24,0},{1,25},{9,17},{17,9},{25,1},{2,26},{10... | collective-permute-start | bytes 442376 | tf_op jit(solution)/shard_map/ppermute | solution.py:249
  49.8 14.0 %collective-permute-start.35 = (bf16[6,4,24,128]{3,2,0,1:T(8,128)(2,1)S(1)}, bf16[6,4,24,128]{3,2,0,1:T(8,128)(2,1)S(1)}, u32[]{:S(2)}, u32[]{:S(2)}) collective-permute-start(bf16[6,4,24,128]{3,2,0,1:T(8,128)(2,1)S(1)} %pad_maximum_fusion.12), channel_id=1, source_target_pairs={{0,16},{8,24},{16,0},{24,8},{1,17},{9,25},{17,1},{25,9},{2,18},{10... | collective-permute-start | bytes 442376 | tf_op jit(solution)/shard_map/ppermute | solution.py:249
  59.2 73.5 %collective-permute-start.13 = (bf16[3,384,128]{2,1,0:T(8,128)(2,1)S(1)}, bf16[3,384,128]{2,1,0:T(8,128)(2,1)S(1)}, u32[]{:S(2)}, u32[]{:S(2)}) collective-permute-start(bf16[3,384,128]{2,1,0:T(8,128)(2,1)S(1)} %bitcast.438), channel_id=1, source_target_pairs={{0,5},{1,4},{4,1},{5,0},{2,7},{3,6},{6,3},{7,2},{8,13},{9,12},{12,... | collective-permute-start | bytes 884744 | tf_op jit(solution)/shard_map/ppermute | solution.py:249
  61.2 71.6 %collective-permute-start.14 = (bf16[3,384,128]{2,1,0:T(8,128)(2,1)S(1)}, bf16[3,384,128]{2,1,0:T(8,128)(2,1)S(1)}, u32[]{:S(2)}, u32[]{:S(2)}) collective-permute-start(bf16[3,384,128]{2,1,0:T(8,128)(2,1)S(1)} %bitcast.439), channel_id=1, source_target_pairs={{0,4},{1,5},{4,0},{5,1},{2,6},{3,7},{6,2},{7,3},{8,12},{9,13},{12,... | collective-permute-start | bytes 884744 | tf_op jit(solution)/shard_map/ppermute | solution.py:249
  62.0 23.7 %collective-permute-start.43 = (bf16[4,6,4,24,128]{4,3,1,2,0:T(8,128)(2,1)S(1)}, bf16[4,6,4,24,128]{4,3,1,2,0:T(8,128)(2,1)S(1)}, u32[]{:S(2)}, u32[]{:S(2)}) collective-permute-start(bf16[4,6,4,24,128]{4,3,1,2,0:T(8,128)(2,1)S(1)} %pad_maximum_fusion.9), channel_id=1, source_target_pairs={{0,24},{8,16},{16,8},{24,0},{1,25},{9,17},{17,9},{25,1},{2,26},{10... | collective-permute-start | bytes 1769480 | tf_op jit(solution)/shard_map/ppermute | solution.py:249
  63.8 25.3 %collective-permute-start.44 = (bf16[4,6,4,24,128]{4,3,1,2,0:T(8,128)(2,1)S(1)}, bf16[4,6,4,24,128]{4,3,1,2,0:T(8,128)(2,1)S(1)}, u32[]{:S(2)}, u32[]{:S(2)}) collective-permute-start(bf16[4,6,4,24,128]{4,3,1,2,0:T(8,128)(2,1)S(1)} %pad_maximum_fusion.9), channel_id=1, source_target_pairs={{0,16},{8,24},{16,0},{24,8},{1,17},{9,25},{17,1},{25,9},{2,18},{10... | collective-permute-start | bytes 1769480 | tf_op jit(solution)/shard_map/ppermute | solution.py:249
  64.6 26.6 %collective-permute-start.45 = (bf16[4,6,4,24,128]{4,3,1,2,0:T(8,128)(2,1)S(1)}, bf16[4,6,4,24,128]{4,3,1,2,0:T(8,128)(2,1)S(1)}, u32[]{:S(2)}, u32[]{:S(2)}) collective-permute-start(bf16[4,6,4,24,128]{4,3,1,2,0:T(8,128)(2,1)S(1)} %pad_maximum_fusion.9), channel_id=1, source_target_pairs={{0,8},{8,0},{16,24},{24,16},{1,9},{9,1},{17,25},{25,17},{2,10},{10... | collective-permute-start | bytes 1769480 | tf_op jit(solution)/shard_map/ppermute | solution.py:249
  85.7 28.1 %collective-permute-start.37 = (bf16[6,384,128]{2,1,0:T(8,128)(2,1)S(1)}, bf16[6,384,128]{2,1,0:T(8,128)(2,1)S(1)}, u32[]{:S(2)}, u32[]{:S(2)}) collective-permute-start(bf16[6,384,128]{2,1,0:T(8,128)(2,1)S(1)} %bitcast.433), channel_id=1, source_target_pairs={{0,5},{1,4},{4,1},{5,0},{2,7},{3,6},{6,3},{7,2},{8,13},{9,12},{12,... | collective-permute-start | bytes 1769480 | tf_op jit(solution)/shard_map/ppermute | solution.py:249
  89.1 28.6 %collective-permute-start.38 = (bf16[6,384,128]{2,1,0:T(8,128)(2,1)S(1)}, bf16[6,384,128]{2,1,0:T(8,128)(2,1)S(1)}, u32[]{:S(2)}, u32[]{:S(2)}) collective-permute-start(bf16[6,384,128]{2,1,0:T(8,128)(2,1)S(1)} %bitcast.434), channel_id=1, source_target_pairs={{0,4},{1,5},{4,0},{5,1},{2,6},{3,7},{6,2},{7,3},{8,12},{9,13},{12,... | collective-permute-start | bytes 1769480 | tf_op jit(solution)/shard_map/ppermute | solution.py:249
  91.2 26.5 %collective-permute-start.39 = (bf16[6,384,128]{2,1,0:T(8,128)(2,1)S(1)}, bf16[6,384,128]{2,1,0:T(8,128)(2,1)S(1)}, u32[]{:S(2)}, u32[]{:S(2)}) collective-permute-start(bf16[6,384,128]{2,1,0:T(8,128)(2,1)S(1)} %bitcast.435), channel_id=1, source_target_pairs={{0,1},{1,0},{4,5},{5,4},{2,3},{3,2},{6,7},{7,6},{8,9},{9,8},{12,13... | collective-permute-start | bytes 1769480 | tf_op jit(solution)/shard_map/ppermute | solution.py:249
  113.8 16.6 %collective-permute-start.19 = (bf16[4,3,4,24,128]{4,3,1,2,0:T(8,128)(2,1)S(1)}, bf16[4,3,4,24,128]{4,3,1,2,0:T(8,128)(2,1)S(1)}, u32[]{:S(2)}, u32[]{:S(2)}) collective-permute-start(bf16[4,3,4,24,128]{4,3,1,2,0:T(8,128)(2,1)S(1)} %pad_maximum_fusion.11), channel_id=1, source_target_pairs={{0,24},{8,16},{16,8},{24,0},{1,25},{9,17},{17,9},{25,1},{2,26},{10... | collective-permute-start | bytes 884744 | tf_op jit(solution)/shard_map/ppermute | solution.py:249
  117.7 12.7 %collective-permute-start.20 = (bf16[4,3,4,24,128]{4,3,1,2,0:T(8,128)(2,1)S(1)}, bf16[4,3,4,24,128]{4,3,1,2,0:T(8,128)(2,1)S(1)}, u32[]{:S(2)}, u32[]{:S(2)}) collective-permute-start(bf16[4,3,4,24,128]{4,3,1,2,0:T(8,128)(2,1)S(1)} %pad_maximum_fusion.11), channel_id=1, source_target_pairs={{0,16},{8,24},{16,0},{24,8},{1,17},{9,25},{17,1},{25,9},{2,18},{10... | collective-permute-start | bytes 884744 | tf_op jit(solution)/shard_map/ppermute | solution.py:249
  117.7 14.4 %collective-permute-start.21 = (bf16[4,3,4,24,128]{4,3,1,2,0:T(8,128)(2,1)S(1)}, bf16[4,3,4,24,128]{4,3,1,2,0:T(8,128)(2,1)S(1)}, u32[]{:S(2)}, u32[]{:S(2)}) collective-permute-start(bf16[4,3,4,24,128]{4,3,1,2,0:T(8,128)(2,1)S(1)} %pad_maximum_fusion.11), channel_id=1, source_target_pairs={{0,8},{8,0},{16,24},{24,16},{1,9},{9,1},{17,25},{25,17},{2,10},{10... | collective-permute-start | bytes 884744 | tf_op jit(solution)/shard_map/ppermute | solution.py:249
  130.4 40.1 %collective-permute-start.46 = (bf16[4,6,768,128]{3,2,1,0:T(8,128)(2,1)}, bf16[4,6,768,128]{3,2,1,0:T(8,128)(2,1)}, u32[]{:S(2)}, u32[]{:S(2)}) collective-permute-start(bf16[4,6,768,128]{3,2,1,0:T(8,128)(2,1)} %pad_maximum_fusion.2), channel_id=1, source_target_pairs={{0,2},{2,0},{1,3},{3,1},{4,6},{6,4},{5,7},{7,5},{8,10},{10,8},{9,1... | collective-permute-start | bytes 14155784 | tf_op jit(solution)/shard_map/ppermute | solution.py:249
  242.3 63.6 %collective-permute-start.57 = (bf16[4,3,768,128]{3,2,1,0:T(8,128)(2,1)}, bf16[4,3,768,128]{3,2,1,0:T(8,128)(2,1)}, u32[]{:S(2)}, u32[]{:S(2)}) collective-permute-start(bf16[4,3,768,128]{3,2,1,0:T(8,128)(2,1)} %dynamic-slice_bitcast_fusion.1), channel_id=1, source_target_pairs={{0,2},{2,0},{1,3},{3,1},{4,6},{6,4},{5,7},{7,5},{8,10},{10,8},{9,1... | collective-permute-start | bytes 7077896 | tf_op jit(solution)/shard_map/ppermute | solution.py:249
  247.7 97.1 %collective-permute-start.80 = (bf16[4,6,768,128]{3,2,1,0:T(8,128)(2,1)}, bf16[4,6,768,128]{3,2,1,0:T(8,128)(2,1)}, u32[]{:S(2)}, u32[]{:S(2)}) collective-permute-start(bf16[4,6,768,128]{3,2,1,0:T(8,128)(2,1)} %dynamic-slice_bitcast_fusion), channel_id=1, source_target_pairs={{0,2},{2,0},{1,3},{3,1},{4,6},{6,4},{5,7},{7,5},{8,10},{10,8},{9,1... | collective-permute-start | bytes 14155784 | tf_op jit(solution)/shard_map/ppermute | solution.py:249
  248.4 49.3 %collective-permute-start.47 = (bf16[512,768]{1,0:T(8,128)(2,1)S(1)}, bf16[512,768]{1,0:T(8,128)(2,1)}, u32[]{:S(2)}, u32[]{:S(2)}) collective-permute-start(bf16[512,768]{1,0:T(8,128)(2,1)S(1)} %copy-done.21), channel_id=1, source_target_pairs={{0,1},{1,0},{2,3},{3,2},{4,5},{5,4},{6,7},{7,6},{8,9},{9,8},{10,11... | collective-permute-start | bytes 2359304 | tf_op jit(solution)/shard_map/ppermute | solution.py:249
  253.2 15.1 %collective-permute-start.50 = (f32[72,128]{1,0:T(8,128)S(1)}, f32[72,128]{1,0:T(8,128)S(1)}, u32[]{:S(2)}, u32[]{:S(2)}) collective-permute-start(f32[72,128]{1,0:T(8,128)S(1)} %fusion.96), channel_id=1, source_target_pairs={{0,1},{1,0},{2,3},{3,2},{4,5},{5,4},{6,7},{7,6},{8,9},{9,8},{10,11... | collective-permute-start | bytes 110600 | tf_op jit(solution)/shard_map/ppermute | solution.py:249
  291.8 12.8 %collective-permute-start.48 = (bf16[512,768]{1,0:T(8,128)(2,1)S(1)}, bf16[512,768]{1,0:T(8,128)(2,1)}, u32[]{:S(2)}, u32[]{:S(2)}) collective-permute-start(bf16[512,768]{1,0:T(8,128)(2,1)S(1)} %convert_element_type.240), channel_id=1, source_target_pairs={{0,1},{1,0},{2,3},{3,2},{4,5},{5,4},{6,7},{7,6},{8,9},{9,8},{10,11... | collective-permute-start | bytes 2359304 | tf_op jit(solution)/shard_map/ppermute | solution.py:249
  310.8 10.4 %collective-permute-start.60 = (bf16[3,384,128]{2,1,0:T(8,128)(2,1)S(1)}, bf16[3,384,128]{2,1,0:T(8,128)(2,1)S(1)}, u32[]{:S(2)}, u32[]{:S(2)}) collective-permute-start(bf16[3,384,128]{2,1,0:T(8,128)(2,1)S(1)} %get-tuple-element.104), channel_id=1, source_target_pairs={{0,5},{1,4},{4,1},{5,0},{2,7},{3,6},{6,3},{7,2},{8,13},{9,12},{12,... | collective-permute-start | bytes 884744 | tf_op jit(solution)/shard_map/ppermute | solution.py:249
  315.9 10.6 %collective-permute-start.65 = (bf16[4,3,4,24,128]{4,3,2,1,0:T(8,128)(2,1)S(1)}, bf16[4,3,4,24,128]{4,3,2,1,0:T(8,128)(2,1)S(1)}, u32[]{:S(2)}, u32[]{:S(2)}) collective-permute-start(bf16[4,3,4,24,128]{4,3,2,1,0:T(8,128)(2,1)S(1)} %get-tuple-element.108), channel_id=1, source_target_pairs={{0,16},{8,24},{16,0},{24,8},{1,17},{9,25},{17,1},{25,9},{2,18},{10... | collective-permute-start | bytes 884744 | tf_op jit(solution)/shard_map/ppermute | solution.py:249
  319.1 10.7 %collective-permute-start.66 = (bf16[4,3,4,24,128]{4,3,2,1,0:T(8,128)(2,1)S(1)}, bf16[4,3,4,24,128]{4,3,2,1,0:T(8,128)(2,1)S(1)}, u32[]{:S(2)}, u32[]{:S(2)}) collective-permute-start(bf16[4,3,4,24,128]{4,3,2,1,0:T(8,128)(2,1)S(1)} %get-tuple-element.107), channel_id=1, source_target_pairs={{0,24},{8,16},{16,8},{24,0},{1,25},{9,17},{17,9},{25,1},{2,26},{10... | collective-permute-start | bytes 884744 | tf_op jit(solution)/shard_map/ppermute | solution.py:249
  321.5 11.4 %collective-permute-start.62 = (bf16[3,4,24,128]{3,2,1,0:T(8,128)(2,1)S(1)}, bf16[3,4,24,128]{3,2,1,0:T(8,128)(2,1)S(1)}, u32[]{:S(2)}, u32[]{:S(2)}) collective-permute-start(bf16[3,4,24,128]{3,2,1,0:T(8,128)(2,1)S(1)} %get-tuple-element.136), channel_id=1, source_target_pairs={{0,16},{8,24},{16,0},{24,8},{1,17},{9,25},{17,1},{25,9},{2,18},{10... | collective-permute-start | bytes 221192 | tf_op jit(solution)/shard_map/ppermute | solution.py:249
  337.8 12.2 %collective-permute-start.70 = (bf16[3,24,128]{2,1,0:T(8,128)(2,1)S(1)}, bf16[3,24,128]{2,1,0:T(8,128)(2,1)S(1)}, u32[]{:S(2)}, u32[]{:S(2)}) collective-permute-start(bf16[3,24,128]{2,1,0:T(8,128)(2,1)S(1)} %get-tuple-element.151), channel_id=1, source_target_pairs={{0,32},{32,0},{64,96},{96,64},{128,160},{160,128},{192,224},{224,1... | collective-permute-start | bytes 55304 | tf_op jit(solution)/shard_map/ppermute | solution.py:249
  338.6 14.8 %collective-permute-start.71 = (bf16[3,24,128]{2,1,0:T(8,128)(2,1)S(1)}, bf16[3,24,128]{2,1,0:T(8,128)(2,1)S(1)}, u32[]{:S(2)}, u32[]{:S(2)}) collective-permute-start(bf16[3,24,128]{2,1,0:T(8,128)(2,1)S(1)} %get-tuple-element.152), channel_id=1, source_target_pairs={{0,64},{32,96},{64,0},{96,32},{128,192},{160,224},{192,128},{224,1... | collective-permute-start | bytes 55304 | tf_op jit(solution)/shard_map/ppermute | solution.py:249
  339.8 15.6 %collective-permute-start.72 = (bf16[3,24,128]{2,1,0:T(8,128)(2,1)S(1)}, bf16[3,24,128]{2,1,0:T(8,128)(2,1)S(1)}, u32[]{:S(2)}, u32[]{:S(2)}) collective-permute-start(bf16[3,24,128]{2,1,0:T(8,128)(2,1)S(1)} %get-tuple-element.153), channel_id=1, source_target_pairs={{0,96},{32,64},{64,32},{96,0},{128,224},{160,192},{192,160},{224,1... | collective-permute-start | bytes 55304 | tf_op jit(solution)/shard_map/ppermute | solution.py:249
  341.4 13.9 %collective-permute-start.73 = (bf16[3,24,128]{2,1,0:T(8,128)(2,1)S(1)}, bf16[3,24,128]{2,1,0:T(8,128)(2,1)S(1)}, u32[]{:S(2)}, u32[]{:S(2)}) collective-permute-start(bf16[3,24,128]{2,1,0:T(8,128)(2,1)S(1)} %get-tuple-element.154), channel_id=1, source_target_pairs={{0,128},{32,160},{64,192},{96,224},{128,0},{160,32},{192,64},{224,... | collective-permute-start | bytes 55304 | tf_op jit(solution)/shard_map/ppermute | solution.py:249
  344.9 10.5 %collective-permute-start.74 = (bf16[3,24,128]{2,1,0:T(8,128)(2,1)S(1)}, bf16[3,24,128]{2,1,0:T(8,128)(2,1)S(1)}, u32[]{:S(2)}, u32[]{:S(2)}) collective-permute-start(bf16[3,24,128]{2,1,0:T(8,128)(2,1)S(1)} %get-tuple-element.155), channel_id=1, source_target_pairs={{0,160},{32,128},{64,224},{96,192},{128,32},{160,0},{192,96},{224,... | collective-permute-start | bytes 55304 | tf_op jit(solution)/shard_map/ppermute | solution.py:249
  355.4 34.9 %collective-permute-start.81 = (bf16[6,384,128]{2,1,0:T(8,128)(2,1)}, bf16[6,384,128]{2,1,0:T(8,128)(2,1)}, u32[]{:S(2)}, u32[]{:S(2)}) collective-permute-start(bf16[6,384,128]{2,1,0:T(8,128)(2,1)} %get-tuple-element.84), channel_id=1, source_target_pairs={{0,1},{1,0},{4,5},{5,4},{2,3},{3,2},{6,7},{7,6},{8,9},{9,8},{12,13... | collective-permute-start | bytes 1769480 | tf_op jit(solution)/shard_map/ppermute | solution.py:249
  357.4 26.1 %collective-permute-start.77 = (bf16[3,6,128]{2,1,0:T(8,128)(2,1)S(1)}, bf16[3,6,128]{2,1,0:T(8,128)(2,1)S(1)}, u32[]{:S(2)}, u32[]{:S(2)}) collective-permute-start(bf16[3,6,128]{2,1,0:T(8,128)(2,1)S(1)} %get-tuple-element.203), channel_id=1, source_target_pairs={{0,6},{2,4},{4,2},{6,0},{1,7},{3,5},{5,3},{7,1},{8,14},{10,12},{12... | collective-permute-start | bytes 13832 | tf_op jit(solution)/shard_map/ppermute | solution.py:249
  372.2 21.2 %collective-permute-start.82 = (bf16[6,384,128]{2,1,0:T(8,128)(2,1)}, bf16[6,384,128]{2,1,0:T(8,128)(2,1)S(1)}, u32[]{:S(2)}, u32[]{:S(2)}) collective-permute-start(bf16[6,384,128]{2,1,0:T(8,128)(2,1)} %get-tuple-element.86), channel_id=1, source_target_pairs={{0,4},{1,5},{4,0},{5,1},{2,6},{3,7},{6,2},{7,3},{8,12},{9,13},{12,... | collective-permute-start | bytes 1769480 | tf_op jit(solution)/shard_map/ppermute | solution.py:249
  374.5 28.0 %collective-permute-start.83 = (bf16[6,384,128]{2,1,0:T(8,128)(2,1)}, bf16[6,384,128]{2,1,0:T(8,128)(2,1)S(1)}, u32[]{:S(2)}, u32[]{:S(2)}) collective-permute-start(bf16[6,384,128]{2,1,0:T(8,128)(2,1)} %get-tuple-element.85), channel_id=1, source_target_pairs={{0,5},{1,4},{4,1},{5,0},{2,7},{3,6},{6,3},{7,2},{8,13},{9,12},{12,... | collective-permute-start | bytes 1769480 | tf_op jit(solution)/shard_map/ppermute | solution.py:249
  377.8 11.7 %collective-permute-start.78 = (bf16[3,6,128]{2,1,0:T(8,128)(2,1)S(1)}, bf16[3,6,128]{2,1,0:T(8,128)(2,1)S(1)}, u32[]{:S(2)}, u32[]{:S(2)}) collective-permute-start(bf16[3,6,128]{2,1,0:T(8,128)(2,1)S(1)} %get-tuple-element.202), channel_id=1, source_target_pairs={{0,4},{2,6},{4,0},{6,2},{1,5},{3,7},{5,1},{7,3},{8,12},{10,14},{12... | collective-permute-start | bytes 13832 | tf_op jit(solution)/shard_map/ppermute | solution.py:249
  389.5 15.1 %collective-permute-start.87 = (bf16[4,6,4,24,128]{4,3,2,1,0:T(8,128)(2,1)S(1)}, bf16[4,6,4,24,128]{4,3,2,1,0:T(8,128)(2,1)S(1)}, u32[]{:S(2)}, u32[]{:S(2)}) collective-permute-start(bf16[4,6,4,24,128]{4,3,2,1,0:T(8,128)(2,1)S(1)} %get-tuple-element.87), channel_id=1, source_target_pairs={{0,8},{8,0},{16,24},{24,16},{1,9},{9,1},{17,25},{25,17},{2,10},{10... | collective-permute-start | bytes 1769480 | tf_op jit(solution)/shard_map/ppermute | solution.py:249
  389.5 23.1 %collective-permute-start.88 = (bf16[4,6,4,24,128]{4,3,2,1,0:T(8,128)(2,1)S(1)}, bf16[4,6,4,24,128]{4,3,2,1,0:T(8,128)(2,1)S(1)}, u32[]{:S(2)}, u32[]{:S(2)}) collective-permute-start(bf16[4,6,4,24,128]{4,3,2,1,0:T(8,128)(2,1)S(1)} %get-tuple-element.89), channel_id=1, source_target_pairs={{0,16},{8,24},{16,0},{24,8},{1,17},{9,25},{17,1},{25,9},{2,18},{10... | collective-permute-start | bytes 1769480 | tf_op jit(solution)/shard_map/ppermute | solution.py:249
  390.3 22.4 %collective-permute-start.89 = (bf16[4,6,4,24,128]{4,3,2,1,0:T(8,128)(2,1)S(1)}, bf16[4,6,4,24,128]{4,3,2,1,0:T(8,128)(2,1)S(1)}, u32[]{:S(2)}, u32[]{:S(2)}) collective-permute-start(bf16[4,6,4,24,128]{4,3,2,1,0:T(8,128)(2,1)S(1)} %get-tuple-element.88), channel_id=1, source_target_pairs={{0,24},{8,16},{16,8},{24,0},{1,25},{9,17},{17,9},{25,1},{2,26},{10... | collective-permute-start | bytes 1769480 | tf_op jit(solution)/shard_map/ppermute | solution.py:249
  404.1 16.9 %collective-permute-start.84 = (bf16[6,4,24,128]{3,2,1,0:T(8,128)(2,1)S(1)}, bf16[6,4,24,128]{3,2,1,0:T(8,128)(2,1)S(1)}, u32[]{:S(2)}, u32[]{:S(2)}) collective-permute-start(bf16[6,4,24,128]{3,2,1,0:T(8,128)(2,1)S(1)} %get-tuple-element.116), channel_id=1, source_target_pairs={{0,8},{8,0},{16,24},{24,16},{1,9},{9,1},{17,25},{25,17},{2,10},{10... | collective-permute-start | bytes 442376 | tf_op jit(solution)/shard_map/ppermute | solution.py:249
  404.2 17.1 %collective-permute-start.85 = (bf16[6,4,24,128]{3,2,1,0:T(8,128)(2,1)S(1)}, bf16[6,4,24,128]{3,2,1,0:T(8,128)(2,1)S(1)}, u32[]{:S(2)}, u32[]{:S(2)}) collective-permute-start(bf16[6,4,24,128]{3,2,1,0:T(8,128)(2,1)S(1)} %get-tuple-element.118), channel_id=1, source_target_pairs={{0,16},{8,24},{16,0},{24,8},{1,17},{9,25},{17,1},{25,9},{2,18},{10... | collective-permute-start | bytes 442376 | tf_op jit(solution)/shard_map/ppermute | solution.py:249
  404.7 18.6 %collective-permute-start.86 = (bf16[6,4,24,128]{3,2,1,0:T(8,128)(2,1)S(1)}, bf16[6,4,24,128]{3,2,1,0:T(8,128)(2,1)S(1)}, u32[]{:S(2)}, u32[]{:S(2)}) collective-permute-start(bf16[6,4,24,128]{3,2,1,0:T(8,128)(2,1)S(1)} %get-tuple-element.117), channel_id=1, source_target_pairs={{0,24},{8,16},{16,8},{24,0},{1,25},{9,17},{17,9},{25,1},{2,26},{10... | collective-permute-start | bytes 442376 | tf_op jit(solution)/shard_map/ppermute | solution.py:249
  413.1 10.3 %collective-permute-start.90 = (bf16[6,4,24,128]{3,2,1,0:T(8,128)(2,1)S(1)}, bf16[6,4,24,128]{3,2,1,0:T(8,128)(2,1)S(1)}, u32[]{:S(2)}, u32[]{:S(2)}) collective-permute-start(bf16[6,4,24,128]{3,2,1,0:T(8,128)(2,1)S(1)} %get-tuple-element.119), channel_id=1, source_target_pairs={{0,1},{1,0},{4,5},{5,4},{2,3},{3,2},{6,7},{7,6},{8,9},{9,8},{12,13... | collective-permute-start | bytes 442376 | tf_op jit(solution)/shard_map/ppermute | solution.py:249
  427.1 10.4 %collective-permute-start.94 = (bf16[6,24,128]{2,1,0:T(8,128)(2,1)S(1)}, bf16[6,24,128]{2,1,0:T(8,128)(2,1)S(1)}, u32[]{:S(2)}, u32[]{:S(2)}) collective-permute-start(bf16[6,24,128]{2,1,0:T(8,128)(2,1)S(1)} %get-tuple-element.129), channel_id=1, source_target_pairs={{0,64},{32,96},{64,0},{96,32},{128,192},{160,224},{192,128},{224,1... | collective-permute-start | bytes 110600 | tf_op jit(solution)/shard_map/ppermute | solution.py:249
  441.6 15.7 %collective-permute-start.100 = (bf16[6,6,128]{2,1,0:T(8,128)(2,1)S(1)}, bf16[6,6,128]{2,1,0:T(8,128)(2,1)S(1)}, u32[]{:S(2)}, u32[]{:S(2)}) collective-permute-start(bf16[6,6,128]{2,1,0:T(8,128)(2,1)S(1)} %get-tuple-element.182), channel_id=1, source_target_pairs={{0,6},{2,4},{4,2},{6,0},{1,7},{3,5},{5,3},{7,1},{8,14},{10,12},{12... | collective-permute-start | bytes 27656 | tf_op jit(solution)/shard_map/ppermute | solution.py:249
  (92 other events, 745.0 us)
